TPU v7x, 256 devices: a whole 4x4x8 slice. The times are simulated.
256 devices in a mesh: blk: 64 (over x, z, y_lo), lat: 4 (over y_hi, core).
Axes of the slice: x: 4, y: 4 (y_hi: 2, y_lo: 2; y = y_hi * 2 + y_lo), z: 8, core: 2. Of those that a mesh axis runs over, the one named last changes fastest.
Arguments:
- displacement: float32 [3, 5, 5, 5, 64, 8, 128], P(None, None, None, None, 'blk', 'lat'), may hold values from -6 to 6
- velocity: float32 [3, 5, 5, 5, 64, 8, 128], P(None, None, None, None, 'blk', 'lat'), may hold values from -6 to 6
- rigidity: float32 [5, 5, 5, 64, 8, 128], P(None, None, None, 'blk', 'lat'), may hold values from 0.5 to 2
- density: float32 [5, 5, 5, 64, 8, 128], P(None, None, None, 'blk', 'lat'), may hold values from 0.5 to 2
- history: float32 [256, 63, 3, 128], P(('blk', 'lat')), may hold values from -0.12 to 0.12
- kernel: float32 [64, 3, 3, 128], replicated, may hold values from -0.4375 to 0.4375
- owner_order: int32 [256], replicated, may hold values from 0 to 255, each once
- rigid_offset: float32 [3], replicated, may hold values from -1.8 to 1.8
- rigid_velocity: float32 [3], replicated, may hold values from -6 to 6
Outputs:
- new_displacement: float32 [3, 5, 5, 5, 64, 8, 128], P(None, None, None, None, 'blk', 'lat')
- new_velocity: float32 [3, 5, 5, 5, 64, 8, 128], P(None, None, None, None, 'blk', 'lat')
- new_history: float32 [256, 63, 3, 128], P(('blk', 'lat'))
- new_offset: float32 [3], replicated
- new_rigid_velocity: float32 [3], replicated
Inputs may be any that keep to these rules, and one draw needn't show every extreme that they name: owner_order names every column 0 to 255 once; row j of history belongs to column owner_order[j].
All inputs are finite; a program needn't handle non-finite values.
Results may differ from a plain program's by a relative error of at most 0.0003.
Values sent between devices are 32-bit elements; how exact they have to be, the bound alone decides.
A program may use at most 64 MiB of HBM per device.

v0:
```python
import functools
import math
import jax
import jax.numpy as jnp
import numpy as np
from jax import lax
from jax.sharding import Mesh
from jax.sharding import PartitionSpec as P

STEPS = 3
BLK = ("blk_0", "blk_1", "blk_2")
LAT = ("lat_0", "lat_1")
BLK_LAT = ("blk_0", "blk_1", "blk_2", "lat_0", "lat_1")
pole_gap = 0.1
time_step = 0.03
rigid_gain = 20.0
coupling = 1.0
highest = lax.Precision.HIGHEST


def with_halo(block, sides, width, periodic):
    for axis, dim in sides:
        count = lax.axis_size(axis)
        forward = [(i, i + 1) for i in range(count - 1)]
        if periodic:
            forward.append((count - 1, 0))
        backward = [(target, source) for source, target in forward]
        low = lax.ppermute(
            lax.slice_in_dim(block, block.shape[dim] - width, None, axis=dim), axis, forward
        )
        high = lax.ppermute(lax.slice_in_dim(block, 0, width, axis=dim), axis, backward)
        block = jnp.concatenate([low, block, high], axis=dim)
    return block


def cut_along(shard, dim, length):
    lengths = shard.shape
    parts = shard.reshape(*lengths[:dim], length, lengths[dim] // length, *lengths[dim + 1 :])
    return jnp.moveaxis(parts, dim, 0)


def sum_at_owner(shard, axis, dim):
    parts = cut_along(shard, dim, lax.axis_size(axis))
    arrived = lax.all_to_all(parts, axis, split_axis=0, concat_axis=0, tiled=True)
    return arrived.sum(axis=0)


def over_axes(shard, axes):
    return functools.reduce(lax.psum, axes, shard)


def node_tables():
    points = np.array([-1.0, -math.sqrt(3.0 / 7.0), 0.0, math.sqrt(3.0 / 7.0), 1.0])
    weights = np.array([0.1, 49.0 / 90.0, 32.0 / 45.0, 49.0 / 90.0, 0.1])
    products = np.array(
        [
            np.prod([points[row_at] - points[others] for others in range(5) if others != row_at])
            for row_at in range(5)
        ]
    )
    slopes = np.zeros((5, 5))
    for row_at in range(5):
        for col_at in range(5):
            if row_at == col_at:
                slopes[row_at, col_at] = sum(
                    (
                        1.0 / (points[row_at] - points[others])
                        for others in range(5)
                        if others != row_at
                    )
                )
            else:
                slopes[row_at, col_at] = (
                    products[row_at] / products[col_at] / (points[row_at] - points[col_at])
                )
    return (points, weights, slopes)


def node_volume():
    points, weights, slopes = node_tables()
    node_weight = jnp.asarray(weights, dtype=jnp.float32)
    volume = node_weight[:, None, None] * node_weight[None, :, None] * node_weight[None, None, :]
    return volume[:, :, :, None, None, None]


def stiffness(values, rigidity):
    points, weights, slopes = node_tables()
    deriv = jnp.asarray(slopes, dtype=jnp.float32)
    scaled = (node_volume() * rigidity)[None]
    first_dir = jnp.einsum("ia,kabcxyz->kibcxyz", deriv, values, precision=highest) * scaled
    second_dir = jnp.einsum("jb,kabcxyz->kajcxyz", deriv, values, precision=highest) * scaled
    third_dir = jnp.einsum("lc,kabcxyz->kablxyz", deriv, values, precision=highest) * scaled
    result = jnp.einsum("ia,kibcxyz->kabcxyz", deriv, first_dir, precision=highest)
    result = result + jnp.einsum("jb,kajcxyz->kabcxyz", deriv, second_dir, precision=highest)
    return result + jnp.einsum("lc,kablxyz->kabcxyz", deriv, third_dir, precision=highest)


def join_faces(lower, upper, before_first, after_last, axis):
    count = lower.shape[axis]
    earlier = jnp.concatenate(
        (before_first, lax.slice_in_dim(upper, 0, count - 1, axis=axis)), axis=axis
    )
    later = jnp.concatenate((lax.slice_in_dim(lower, 1, count, axis=axis), after_last), axis=axis)
    return (lower + earlier, upper + later)


def assemble(forces):
    lower, upper = (forces[:, 0], forces[:, 4])
    count = lower.shape[3]
    paired = jnp.concatenate((lower, upper), axis=3)
    widened = with_halo(paired, ((BLK, 3),), 1, True)
    lower, upper = join_faces(
        lower,
        upper,
        lax.slice_in_dim(widened, 0, 1, axis=3),
        lax.slice_in_dim(widened, 3, 4, axis=3),
        3,
    )
    forces = forces.at[:, 0].set(lower).at[:, 4].set(upper)
    lower, upper = (forces[:, :, 0], forces[:, :, 4])
    count = lower.shape[4]
    paired = jnp.concatenate(
        (lax.slice_in_dim(lower, 0, 1, axis=4), lax.slice_in_dim(upper, count - 1, count, axis=4)),
        axis=4,
    )
    widened = with_halo(paired, ((LAT, 4),), 1, False)
    lower, upper = join_faces(
        lower,
        upper,
        lax.slice_in_dim(widened, 0, 1, axis=4),
        lax.slice_in_dim(widened, 3, 4, axis=4),
        4,
    )
    forces = forces.at[:, :, 0].set(lower).at[:, :, 4].set(upper)
    lower, upper = (forces[:, :, :, 0], forces[:, :, :, 4])
    empty = jnp.zeros_like(lax.slice_in_dim(lower, 0, 1, axis=5))
    lower, upper = join_faces(lower, upper, empty, empty, 5)
    return forces.at[:, :, :, 0].set(lower).at[:, :, :, 4].set(upper)


def interface_grid(row_first, row_count, col_first, col_count, lat_elems, lon_elems):
    points, weights, slopes = node_tables()
    nodes = jnp.asarray(points, dtype=jnp.float32)
    node_weight = jnp.asarray(weights, dtype=jnp.float32)
    theta_step = (math.pi - 2.0 * pole_gap) / lat_elems
    phi_step = 2.0 * math.pi / lon_elems
    row_elem = (row_first + jnp.arange(5 * row_count, dtype=jnp.int32) // 5).astype(jnp.float32)
    col_elem = (col_first + jnp.arange(5 * col_count, dtype=jnp.int32) // 5).astype(jnp.float32)
    colatitude = pole_gap + (row_elem + 0.5 * (1.0 + jnp.tile(nodes, row_count))) * theta_step
    longitude = (col_elem + 0.5 * (1.0 + jnp.tile(nodes, col_count))) * phi_step
    row_weight = jnp.tile(node_weight, row_count)
    col_weight = jnp.tile(node_weight, col_count)
    area_weight = (
        0.25
        * theta_step
        * phi_step
        * (row_weight * jnp.sin(colatitude))[:, None]
        * col_weight[None, :]
    )
    face_weight = row_weight[:, None] * col_weight[None, :]
    return (colatitude, longitude, area_weight, face_weight)


def rotation(colatitude, longitude):
    sin_theta = jnp.sin(colatitude)[:, None]
    cos_theta = jnp.cos(colatitude)[:, None]
    sin_phi = jnp.sin(longitude)[None, :]
    cos_phi = jnp.cos(longitude)[None, :]
    filled = jnp.ones((colatitude.shape[0], longitude.shape[0]), jnp.float32)
    radial = (sin_theta * cos_phi, sin_theta * sin_phi, cos_theta * filled)
    polar_dir = (cos_theta * cos_phi, cos_theta * sin_phi, -sin_theta * filled)
    azimuth = (-sin_phi * filled, cos_phi * filled, 0.0 * filled)
    return jnp.stack(
        [jnp.stack([radial[axis_at], polar_dir[axis_at], azimuth[axis_at]]) for axis_at in range(3)]
    )


def legendre(colatitude, degrees):
    cosine = jnp.cos(colatitude)[:, None]
    sine = jnp.sin(colatitude)[:, None]
    orders = jnp.arange(degrees, dtype=jnp.float32)[None, :]
    factor = jnp.where(
        orders == 0,
        math.sqrt(0.5),
        -jnp.sqrt((2.0 * orders + 1.0) / jnp.maximum(2.0 * orders, 1.0)) * sine,
    )
    diagonal = jnp.cumprod(factor, axis=1)

    def advance(state_pair, degree):
        previous, before = state_pair
        level = degree.astype(jnp.float32)
        upward = jnp.sqrt(
            jnp.maximum(4.0 * level * level - 1.0, 0.0)
            / jnp.maximum(level * level - orders * orders, 1.0)
        )
        lowered = (level - 1.0) * (level - 1.0)
        downward = jnp.sqrt(
            jnp.maximum(lowered - orders * orders, 0.0) / jnp.maximum(4.0 * lowered - 1.0, 1.0)
        )
        recurred = upward * (cosine * previous - downward * before)
        values = jnp.where(
            orders == level,
            diagonal,
            jnp.where(
                orders + 1.0 == level,
                jnp.sqrt(2.0 * orders + 3.0) * cosine * diagonal,
                jnp.where(orders + 1.0 < level, recurred, 0.0),
            ),
        )
        return ((values, previous), values)

    zeroed = jnp.zeros((colatitude.shape[0], degrees), jnp.float32)
    finals, levels = lax.scan(advance, (zeroed, zeroed), jnp.arange(degrees, dtype=jnp.int32))
    return levels


def doubled(colatitude, degrees):
    levels = legendre(colatitude, degrees)
    return jnp.concatenate((levels, levels), axis=2)


def circle_table(longitude, degrees):
    orders = jnp.arange(degrees, dtype=jnp.float32)[None, :]
    angles = longitude[:, None] * orders
    cosines = jnp.where(
        orders == 0, 1.0 / math.sqrt(2.0 * math.pi), jnp.cos(angles) / math.sqrt(math.pi)
    )
    sines = jnp.where(orders == 0, 0.0, jnp.sin(angles) / math.sqrt(math.pi))
    return jnp.concatenate((cosines, sines), axis=1)


def synthesize(coeffs, circle, levels):
    partial_value = jnp.einsum("ckl,ltc->ktc", coeffs, levels, precision=highest)
    return jnp.einsum("ktc,fc->ktf", partial_value, circle, precision=highest)


def respond(owned_rows, history, kernel):
    stacked = jnp.concatenate((owned_rows[:, None], history), axis=1)
    replies = jnp.einsum("jabl,cjbl->cal", kernel, stacked, precision=highest)
    return (replies, stacked[:, :-1])


def to_grid(values):
    bottom = values[:, :, :, 0, :, :, 0]
    lon_count, lat_count = (bottom.shape[3], bottom.shape[4])
    return bottom.transpose(0, 4, 2, 3, 1).reshape(3, 5 * lat_count, 5 * lon_count)


def from_grid(grid, lon_count, lat_count):
    return grid.reshape(3, lat_count, 5, lon_count, 5).transpose(0, 4, 2, 3, 1)


def on_device(
    displacement,
    velocity,
    rigidity,
    density,
    history,
    kernel,
    owner_order,
    rigid_offset,
    rigid_velocity,
):
    lon_count, lat_count = (displacement.shape[4], displacement.shape[5])
    blk_count, lat_devices = (lax.axis_size(BLK), lax.axis_size(LAT))
    lon_elems, lat_elems = (lon_count * blk_count, lat_count * lat_devices)
    degrees = kernel.shape[3]
    colatitude, longitude, area_weight, face_weight = interface_grid(
        lax.axis_index(LAT) * lat_count,
        lat_count,
        lax.axis_index(BLK) * lon_count,
        lon_count,
        lat_elems,
        lon_elems,
    )
    rotated = rotation(colatitude, longitude)
    levels = doubled(colatitude, degrees)
    circle = circle_table(longitude, degrees)
    inverse = 1.0 / assemble((density * node_volume())[None])
    block_count = 2 * degrees // blk_count
    circle_ordered = jnp.take(circle, owner_order, axis=1)
    block_columns = lax.dynamic_slice_in_dim(
        owner_order, lax.axis_index(BLK) * block_count, block_count, 0
    )
    levels_block = jnp.take(levels, block_columns, axis=2)
    for step_index in range(STEPS):
        relative = to_grid(displacement) - jnp.einsum(
            "jktf,j->ktf", rotated, rigid_offset, precision=highest
        )
        weighted = relative * area_weight
        block_sums = sum_at_owner(
            jnp.einsum("ktf,fc->ckt", weighted, circle_ordered, precision=highest), BLK, 0
        )
        block_partial = jnp.einsum("ckt,ltc->ckl", block_sums, levels_block, precision=highest)
        owned_rows = sum_at_owner(block_partial, LAT, 0)
        replies, history = respond(owned_rows, history, kernel)
        gathered = lax.all_gather(replies, BLK_LAT, axis=0, tiled=True)
        coeffs = jnp.zeros_like(gathered).at[owner_order].set(gathered)
        traction = synthesize(coeffs, circle, levels)
        pull_sum = over_axes(
            jnp.einsum("jktf,ktf->j", rotated * area_weight, traction, precision=highest), BLK_LAT
        )
        rigid_velocity = rigid_velocity + time_step * rigid_gain * pull_sum
        rigid_offset = rigid_offset + time_step * rigid_velocity
        forces = -stiffness(displacement, rigidity)
        forces = forces.at[:, :, :, 0, :, :, 0].add(
            from_grid(-coupling * face_weight * traction, lon_count, lat_count)
        )
        velocity = velocity + time_step * assemble(forces) * inverse
        displacement = displacement + time_step * velocity
    return (displacement, velocity, history, rigid_offset, rigid_velocity)


def solution(mesh):
    split = Mesh(mesh.devices.reshape(4, 8, 2, 2, 2), ("blk_0", "blk_1", "blk_2", "lat_0", "lat_1"))
    in_specs = (
        P(None, None, None, None, BLK, LAT, None),
        P(None, None, None, None, BLK, LAT, None),
        P(None, None, None, BLK, LAT, None),
        P(None, None, None, BLK, LAT, None),
        P(BLK_LAT, None, None, None),
        P(),
        P(),
        P(),
        P(),
    )
    out_specs = (
        P(None, None, None, None, BLK, LAT, None),
        P(None, None, None, None, BLK, LAT, None),
        P(BLK_LAT, None, None, None),
        P(),
        P(),
    )
    return jax.shard_map(
        on_device, mesh=split, in_specs=in_specs, out_specs=out_specs, check_vma=False
    )
```

profile of v0, /device:TPU:1, one launch (start us, length us, event | category | flops | bytes accessed | tf_op | source)
XLA Modules:
  0.0 1690.9 jit_solution(3025484764923406583)
XLA Ops:
  6.8 7.5 collective-permute-start.5
  24.4 6.4 all-to-all-start
  32.6 281.5 %while.46 = (s32[]{:T(128)}, f32[10,128]{1,0:T(8,128)S(1)}, f32[10,128]{1,0:T(8,128)S(1)}, f32[128,10,128]{2,1,0:T(8,128)}, s32[128]{0:T(128)S(1)}, /*index=5*/f...) while((s32[]{:T(128)}, f32[10,128]{1,0:T(8,128)S(1)}, ...), condition=%wide.region_2.3_spmd.clone.clone, body=%wide.region_1.2_spmd.clone.clone.sunk | while | flops 14736 | bytes 38715 | solution.py:213
  325.0 6.2 collective-permute-start.6
  333.3 4.5 collective-permute-done.7
  345.5 346.9 %all_gather.9 = f32[256,3,128]{2,1,0:T(4,128)S(1)} all-gather(f32[1,3,128]{2,1,0:T(4,128)S(1)} %bitcast.584), channel_id=1, replica_groups=mesh['blk_0'=4,'blk_1'=8,'blk_2'=2,'lat_0'=2,'lat_1'=2] {'blk_0','blk_1'..., dimensions={0}, use_global_device_ids=true | all-gather | bytes 394752 | tf_op jit(solution)/shard_map/all_gather | solution.py:297
  692.5 7.0 scatter_fusion
  699.5 3.4 convolution_bitcast_fusion.8
  704.7 6.0 psum.105
  710.9 10.7 psum.106
  721.7 3.8 psum.107
  728.2 5.3 psum.108
  733.5 10.0 psum.109
  744.4 4.1 scatter.101
  748.6 4.1 scatter.104
  752.7 7.1 collective-permute-start.2
  763.1 5.7 collective-permute-done.3
  771.8 5.2 all-to-all-start.2
  778.6 10.0 all-to-all-done.2
  789.6 5.0 all-to-all-start.3
  799.3 341.8 %all_gather.10 = f32[256,3,128]{2,1,0:T(4,128)S(1)} all-gather(f32[1,3,128]{2,1,0:T(4,128)S(1)} %bitcast.585), channel_id=1, replica_groups=mesh['blk_0'=4,'blk_1'=8,'blk_2'=2,'lat_0'=2,'lat_1'=2] {'blk_0','blk_1'..., dimensions={0}, use_global_device_ids=true | all-gather | bytes 394752 | tf_op jit(solution)/shard_map/all_gather | solution.py:297
  1141.2 7.0 scatter_fusion.1
  1148.2 3.4 convolution_bitcast_fusion.7
  1153.6 6.1 psum.110
  1161.6 10.7 psum.111
  1174.9 3.9 psum.112
  1180.3 5.6 psum.113
  1188.1 9.8 psum.114
  1203.5 6.0 collective-permute-done.8
  1209.7 4.0 scatter.124
  1213.7 4.0 scatter.125
  1217.7 5.7 collective-permute-start.10
  1225.5 5.0 collective-permute-done.11
  1234.4 4.8 all-to-all-start.4
  1239.9 11.1 all-to-all-done.4
  1258.9 343.5 %all_gather.11 = f32[256,3,128]{2,1,0:T(4,128)S(1)} all-gather(f32[1,3,128]{2,1,0:T(4,128)S(1)} %bitcast.586), channel_id=1, replica_groups=mesh['blk_0'=4,'blk_1'=8,'blk_2'=2,'lat_0'=2,'lat_1'=2] {'blk_0','blk_1'..., dimensions={0}, use_global_device_ids=true | all-gather | bytes 394752 | tf_op jit(solution)/shard_map/all_gather | solution.py:297
  1602.4 7.0 scatter_fusion.2
  1609.5 3.4 convolution_bitcast_fusion.6
  1614.6 6.1 psum.115
  1621.5 10.7 psum.116
  1634.0 3.8 psum.117
  1638.5 5.4 psum.118
  1644.9 9.8 psum.119
  1660.4 7.0 collective-permute-done.12
  1667.6 4.0 scatter.162
  1671.5 4.0 scatter.163
  1675.6 4.2 collective-permute-start.14
  1681.9 5.0 collective-permute-done.15
  (1499 shorter events, 299.8 us)
Async XLA Ops:
  0.6 30.2 %copy-start.20 = (f32[5,5,1,1,1,1]{1,0,5,4,3,2:T(8,128)S(1)}, f32[5,5,1,1,1,1]{1,0,5,4,3,2:T(8,128)}, u32[]{:S(2)}) copy-start(f32[5,5,1,1,1,1]{1,0,5,4,3,2:T(8,128)} %constant.794) | copy-start | bytes 304
  0.6 30.2 %copy-start = (f32[3,5,5,5,1,2,128]{6,5,4,3,2,1,0:T(2,128)S(1)}, f32[3,5,5,5,1,2,128]{6,5,4,3,2,1,0:T(2,128)}, u32[]{:S(2)}) copy-start(f32[3,5,5,5,1,2,128]{6,5,4,3,2,1,0:T(2,128)} %param.74) | copy-start | bytes 1152004
  4.0 27.5 %copy-start.29 = (f32[1,5,5,5,1,2,128]{6,5,3,2,4,1,0:T(2,128)}, f32[1,5,5,5,1,2,128]{6,5,3,2,4,1,0:T(2,128)S(1)}, u32[]{:S(2)}) copy-start(f32[1,5,5,5,1,2,128]{6,5,3,2,4,1,0:T(2,128)S(1)} %get-tuple-element.628) | copy-start | bytes 384004
  4.7 318.7 %collective-permute-start.4 = (f32[1,5,5,1,2,128]{5,4,2,1,3,0:T(2,128)}, f32[1,5,5,1,2,128]{5,4,2,1,3,0:T(2,128)}, u32[]{:S(2)}, u32[]{:S(2)}) collective-permute-start(f32[1,5,5,1,2,128]{5,4,2,1,3,0:T(2,128)} %get-tuple-element.636), channel_id=1, source_target_pairs={{0,4},{4,8},{8,12},{12,16},{16,20},{20,24},{24,28},{28,32},{32,36}... | collective-permute-start | bytes 76808 | tf_op jit(solution)/shard_map/ppermute | solution.py:28
  6.8 317.3 %collective-permute-start.5 = (f32[1,5,5,1,2,128]{5,4,2,1,3,0:T(2,128)S(1)}, f32[1,5,5,1,2,128]{5,4,2,1,3,0:T(2,128)}, u32[]{:S(2)}, u32[]{:S(2)}) collective-permute-start(f32[1,5,5,1,2,128]{5,4,2,1,3,0:T(2,128)S(1)} %get-tuple-element.635), channel_id=1, source_target_pairs={{4,0},{8,4},{12,8},{16,12},{20,16},{24,20},{28,24},{32,28},{36,32}... | collective-permute-start | bytes 76808 | tf_op jit(solution)/shard_map/ppermute | solution.py:31
  15.0 1126.2 %copy-start.33 = (s32[256]{0:T(256)}, s32[256]{0:T(256)S(1)}, u32[]{:S(2)}) copy-start(s32[256]{0:T(256)S(1)} %compare_select_fusion) | copy-start | bytes 3076
  15.7 754.7 %copy-start.44 = (pred[256]{0:T(512)(128)(4,1)}, pred[256]{0:T(512)(128)(4,1)S(1)}, u32[]{:S(2)}) copy-start(pred[256]{0:T(512)(128)(4,1)S(1)} %compare_and_fusion.1) | copy-start | bytes 772
  24.4 313.8 %all-to-all-start = ((f32[64,4,3,10]{3,1,2,0:T(4,128)}), f32[64,4,3,10]{3,1,2,0:T(4,128)S(1)}, u32[]{:S(2)}, u32[]{:S(2)}) async-start(f32[64,4,3,10]{3,1,2,0:T(4,128)} %copy.581), calls=%async_computation | async-start | bytes 786432 | tf_op jit(solution)/shard_map/all_to_all | solution.py:44
  32.2 756.5 %copy-start.39 = (pred[4]{0:T(512)(128)(4,1)}, pred[4]{0:T(512)(128)(4,1)S(1)}, u32[]{:S(2)}) copy-start(pred[4]{0:T(512)(128)(4,1)S(1)} %get-tuple-element.596) | copy-start | bytes 16
  317.6 861.3 %copy-start.1 = (f32[5,5,5,2,128]{4,0,3,2,1:T(8,128)}, f32[5,5,5,2,128]{4,0,3,2,1:T(8,128)S(1)}, u32[]{:S(2)}) copy-start(f32[5,5,5,2,128]{4,0,3,2,1:T(8,128)S(1)} %copy.561) | copy-start | bytes 384004
  321.1 24.2 %copy-start.23 = (f32[1,63,3,128]{3,1,2,0:T(8,128)}, f32[1,63,3,128]{3,1,2,0:T(8,128)S(1)}, u32[]{:S(2)}) copy-start(f32[1,63,3,128]{3,1,2,0:T(8,128)S(1)} %copy.585) | copy-start | bytes 290308
  321.1 24.3 %copy-start.14 = (f32[64,3,3,128]{3,0,2,1:T(8,128)S(1)}, f32[64,3,3,128]{3,0,2,1:T(8,128)}, u32[]{:S(2)}) copy-start(f32[64,3,3,128]{3,0,2,1:T(8,128)} %param.79) | copy-start | bytes 884740
  325.0 8.2 collective-permute-start.6
  331.3 6.5 collective-permute-start.7
  339.1 6.2 all-to-all-start.1
  702.8 57.0 %copy-start.24 = (f32[1,63,3,128]{3,1,2,0:T(8,128)S(1)}, f32[1,63,3,128]{3,1,2,0:T(8,128)}, u32[]{:S(2)}) copy-start(f32[1,63,3,128]{3,1,2,0:T(8,128)} %copy-done.23) | copy-start | bytes 290308
  725.5 23.0 %collective-permute-start.1 = (f32[3,5,5,1,2,128]{5,4,2,1,0,3:T(2,128)S(1)}, f32[3,5,5,1,2,128]{5,4,2,1,0,3:T(2,128)S(1)}, u32[]{:S(2)}, u32[]{:S(2)}) collective-permute-start(f32[3,5,5,1,2,128]{5,4,2,1,0,3:T(2,128)S(1)} %bitcast.558), channel_id=1, source_target_pairs={{4,0},{8,4},{12,8},{16,12},{20,16},{24,20},{28,24},{32,28},{36,32}... | collective-permute-start | bytes 230408 | tf_op jit(solution)/shard_map/ppermute | solution.py:31
  733.5 10.9 collective-permute-start
  752.7 8.4 collective-permute-start.2
  759.9 39.3 %copy-start.25 = (f32[1,63,3,128]{3,1,2,0:T(8,128)}, f32[1,63,3,128]{3,1,2,0:T(8,128)S(1)}, u32[]{:S(2)}) copy-start(f32[1,63,3,128]{3,1,2,0:T(8,128)S(1)} %fusion.99) | copy-start | bytes 290308
  761.2 7.7 collective-permute-start.3
  771.8 27.5 %copy-start.15 = (f32[64,3,3,128]{3,0,2,1:T(8,128)S(1)}, f32[64,3,3,128]{3,0,2,1:T(8,128)}, u32[]{:S(2)}) copy-start(f32[64,3,3,128]{3,0,2,1:T(8,128)} %param.79) | copy-start | bytes 884740
  771.8 16.8 all-to-all-start.2
  789.6 9.6 all-to-all-start.3
  799.2 349.0 %copy-start.37 = (f32[1,1,3,128]{3,1,2,0:T(1,128)}, f32[1,1,3,128]{3,1,2,0:T(1,128)S(1)}, u32[]{:S(2)}) copy-start(f32[1,1,3,128]{3,1,2,0:T(1,128)S(1)} %broadcast_in_dim.183) | copy-start | bytes 4612
  1153.6 32.3 %copy-start.35 = (f32[5,5,1,1,1,1]{1,0,2,4,5,3:T(8,128)S(1)}, f32[5,5,1,1,1,1]{1,0,2,4,5,3:T(8,128)}, u32[]{:S(2)}) copy-start(f32[5,5,1,1,1,1]{1,0,2,4,5,3:T(8,128)} %constant.795) | copy-start | bytes 304
  1174.9 23.0 %copy-start.49 = (f32[3]{0:T(128)S(1)}, f32[3]{0:T(128)}, u32[]{:S(2)}) copy-start(f32[3]{0:T(128)} %param.82) | copy-start | bytes 40
  1174.9 23.0 %copy-start.51 = (f32[3]{0:T(128)S(1)}, f32[3]{0:T(128)}, u32[]{:S(2)}) copy-start(f32[3]{0:T(128)} %copy-done.50) | copy-start | bytes 40
  1174.9 23.0 %copy-start.42 = (f32[3]{0:T(128)S(1)}, f32[3]{0:T(128)}, u32[]{:S(2)}) copy-start(f32[3]{0:T(128)} %copy-done.41) | copy-start | bytes 40
  1180.3 21.8 %copy-start.26 = (f32[1,63,3,128]{3,1,2,0:T(8,128)S(1)}, f32[1,63,3,128]{3,1,2,0:T(8,128)}, u32[]{:S(2)}) copy-start(f32[1,63,3,128]{3,1,2,0:T(8,128)} %copy-done.25) | copy-start | bytes 290308
  1180.3 21.8 %copy-start.38 = (f32[1,1,3,128]{3,1,2,0:T(1,128)S(1)}, f32[1,1,3,128]{3,1,2,0:T(1,128)}, u32[]{:S(2)}) copy-start(f32[1,1,3,128]{3,1,2,0:T(1,128)} %copy-done.37) | copy-start | bytes 4612
  1199.3 4.1 collective-permute-start.9
  1202.0 7.5 collective-permute-start.8
  1202.1 56.6 %copy-start.21 = (f32[1,63,3,128]{3,1,2,0:T(8,128)}, f32[1,63,3,128]{3,1,2,0:T(8,128)S(1)}, u32[]{:S(2)}) copy-start(f32[1,63,3,128]{3,1,2,0:T(8,128)S(1)} %fusion.97) | copy-start | bytes 290308
  1217.7 7.7 collective-permute-start.10
  1223.4 7.0 collective-permute-start.11
  1234.4 24.5 %copy-start.16 = (f32[64,3,3,128]{3,0,2,1:T(8,128)S(1)}, f32[64,3,3,128]{3,0,2,1:T(8,128)}, u32[]{:S(2)}) copy-start(f32[64,3,3,128]{3,0,2,1:T(8,128)} %param.79) | copy-start | bytes 884740
  1234.4 16.7 all-to-all-start.4
  1239.1 363.3 %copy-start.34 = (s32[256]{0:T(256)S(1)}, s32[256]{0:T(256)}, u32[]{:S(2)}) copy-start(s32[256]{0:T(256)} %copy-done.33) | copy-start | bytes 3076
  1252.0 6.7 all-to-all-start.5
  1614.6 29.3 %copy-start.36 = (f32[5,5,1,1,1,1]{1,0,2,4,5,3:T(8,128)S(1)}, f32[5,5,1,1,1,1]{1,0,2,4,5,3:T(8,128)}, u32[]{:S(2)}) copy-start(f32[5,5,1,1,1,1]{1,0,2,4,5,3:T(8,128)} %constant.795) | copy-start | bytes 304
  1634.0 20.7 %copy-start.43 = (f32[3]{0:T(128)S(1)}, f32[3]{0:T(128)}, u32[]{:S(2)}) copy-start(f32[3]{0:T(128)} %copy-done.41) | copy-start | bytes 40
  1634.0 20.7 %copy-start.47 = (f32[3]{0:T(128)S(1)}, f32[3]{0:T(128)}, u32[]{:S(2)}) copy-start(f32[3]{0:T(128)} %copy-done.46) | copy-start | bytes 40
  1638.5 20.3 %copy-start.22 = (f32[1,63,3,128]{3,1,2,0:T(8,128)S(1)}, f32[1,63,3,128]{3,1,2,0:T(8,128)}, u32[]{:S(2)}) copy-start(f32[1,63,3,128]{3,1,2,0:T(8,128)} %copy-done.21) | copy-start | bytes 290308
  1656.2 4.1 collective-permute-start.13
  1659.6 7.8 collective-permute-start.12
  1675.6 6.2 collective-permute-start.14
  1679.8 7.0 collective-permute-start.15
  (27 other events, 136.0 us)
where the time goes:
time: 1700 us; the launch traced here: 1690 us
  blocking collectives  1140 us (67%)
  local copies, waits for them, and re-layouts  163 us (10%)
  other arithmetic  119 us (7%)
  loops' own time  86.9 us (5%)
  starting transfers between devices  76.8 us (5%)
  waiting for transfers between devices  64.3 us (4%)
  matrix products  38.2 us (2%)
    all_gather x3, blocking collectives, on_device(): gathered = lax.all_gather(replies, BLK_LAT, axis=0, tiled=True)  1030 us
    psum x15, blocking collectives, over_axes(): return functools.reduce(lax.psum, axes, shard)  108 us
    another operation x1, loops' own time, legendre(): lax.scan(advance, (zeroed, zeroed), jnp.arange(degrees, dtype=jnp.int32))  86.9 us
    dynamic_update_slice x128, other arithmetic, legendre(): lax.scan(advance, (zeroed, zeroed), jnp.arange(degrees, dtype=jnp.int32))  86.7 us
    dynamic_slice x128, local copies, waits for them, and re-layouts, legendre(): lax.scan(advance, (zeroed, zeroed), jnp.arange(degrees, dtype=jnp.int32))  82.7 us
  transfers between devices with their start and end apart: 22, of which 14 were waited for; matrix products, arithmetic and copies ran while one was open for 14% of the time, Pallas kernels for 0%

commit v1 on v0

--- a/solution.py
+++ b/solution.py
@@ -16,6 +16,13 @@
 rigid_gain = 20.0
 coupling = 1.0
 highest = lax.Precision.HIGHEST
+
+
+def swapped_in(x, mesh_axis, d):
+    size = lax.axis_size(mesh_axis)
+    blocks = jnp.stack([x for _ in range(size)])
+    blocks = lax.all_to_all(blocks, mesh_axis, split_axis=0, concat_axis=0)
+    return jnp.concatenate(blocks, axis=d)
 
 
 def with_halo(block, sides, width, periodic):
@@ -294,7 +301,7 @@
         block_partial = jnp.einsum("ckt,ltc->ckl", block_sums, levels_block, precision=highest)
         owned_rows = sum_at_owner(block_partial, LAT, 0)
         replies, history = respond(owned_rows, history, kernel)
-        gathered = lax.all_gather(replies, BLK_LAT, axis=0, tiled=True)
+        gathered = swapped_in(replies, BLK_LAT, 0)
         coeffs = jnp.zeros_like(gathered).at[owner_order].set(gathered)
         traction = synthesize(coeffs, circle, levels)
         pull_sum = over_axes(

time: 1700 us -> 756 us (0.44)
  blocking collectives: 1140 us -> 131 us
  waiting for transfers between devices: 64.3 us -> 100 us
  starting transfers between devices: 76.8 us -> 95.4 us
    all_gather x3 -> x0, blocking collectives: 1030 us -> none  [on_device(): gathered = lax.all_gather(replies, BLK_LAT, axis=0, tiled=True)]
    all_to_all x0 -> x3, waiting for transfers between devices: none -> 46.7 us  [swapped_in(): blocks = lax.all_to_all(blocks, mesh_axis, split_axis=0, concat_axis=0)]
    all_to_all x0 -> x3, starting transfers between devices: none -> 24.3 us  [swapped_in(): blocks = lax.all_to_all(blocks, mesh_axis, split_axis=0, concat_axis=0)]
    scatter x3, local copies, waits for them, and re-layouts: 20.9 us -> 39.6 us  [on_device(): coeffs = jnp.zeros_like(gathered).at[owner_order].set(gathered)]
  transfers between devices with their start and end apart: 22 -> 24, of which waited for: 14 -> 15; matrix products, arithmetic and copies ran while one was open for 14% -> 30% of each run, Pallas kernels for 0% -> 0%
where the time goes in v1:
time: 756 us; the launch traced here: 743 us
  local copies, waits for them, and re-layouts  174 us (23%)
  blocking collectives  131 us (17%)
  other arithmetic  122 us (16%)
  waiting for transfers between devices  100 us (13%)
  starting transfers between devices  95.4 us (13%)
  loops' own time  75.7 us (10%)
  matrix products  41.9 us (6%)
    psum x15, blocking collectives, over_axes(): return functools.reduce(lax.psum, axes, shard)  115 us
    dynamic_update_slice x128, other arithmetic, legendre(): lax.scan(advance, (zeroed, zeroed), jnp.arange(degrees, dtype=jnp.int32))  86.7 us
    another operation x1, loops' own time, legendre(): lax.scan(advance, (zeroed, zeroed), jnp.arange(degrees, dtype=jnp.int32))  75.7 us
    dynamic_slice x128, local copies, waits for them, and re-layouts, legendre(): lax.scan(advance, (zeroed, zeroed), jnp.arange(degrees, dtype=jnp.int32))  70.3 us
    all_to_all x3, waiting for transfers between devices, swapped_in(): blocks = lax.all_to_all(blocks, mesh_axis, split_axis=0, concat_axis=0)  46.7 us
    scatter x3, local copies, waits for them, and re-layouts, on_device(): coeffs = jnp.zeros_like(gathered).at[owner_order].set(gathered)  39.6 us
    ppermute x8, starting transfers between devices, with_halo(): lax.ppermute(lax.slice_in_dim(block, block.shape[dim] - width, None, axis...  27.8 us
    all_to_all x3, starting transfers between devices, swapped_in(): blocks = lax.all_to_all(blocks, mesh_axis, split_axis=0, concat_axis=0)  24.3 us
  transfers between devices with their start and end apart: 24, of which 15 were waited for; matrix products, arithmetic and copies ran while one was open for 30% of the time, Pallas kernels for 0%

profile of v1, /device:TPU:1, one launch (start us, length us, event | category | flops | bytes accessed | tf_op | source)
XLA Modules:
  0.0 742.6 jit_solution(50296566917709043)
XLA Ops:
  6.8 7.5 %collective-permute-start.5 = (f32[1,5,5,1,2,128]{5,4,2,1,3,0:T(2,128)}, f32[1,5,5,1,2,128]{5,4,2,1,3,0:T(2,128)}, u32[]{:S(2)}, u32[]{:S(2)}) collective-permute-start(f32[1,5,5,1,2,128]{5,4,2,1,3,0:T(2,128)} %get-tuple-element.645), channel_id=1, source_target_pairs={{4,0},{8,4},{12,8},{16,12},{20,16},{24,20},{28,24},{32,28},{36,32}... | collective-permute-start | bytes 76808 | tf_op jit(solution)/shard_map/ppermute | solution.py:38
  25.0 6.4 all-to-all-start
  33.7 258.0 %while.46 = (s32[]{:T(128)}, f32[10,128]{1,0:T(8,128)S(1)}, f32[10,128]{1,0:T(8,128)S(1)}, f32[128,10,128]{2,1,0:T(8,128)}, s32[128]{0:T(128)S(1)}, /*index=5*/f...) while((s32[]{:T(128)}, f32[10,128]{1,0:T(8,128)S(1)}, ...), condition=%wide.region_2.3_spmd.clone.clone, body=%wide.region_1.2_spmd.clone.clone.sunk | while | flops 14736 | bytes 38715 | solution.py:220
  302.5 6.2 collective-permute-start.6
  312.3 4.9 all-to-all-start.1
  317.3 4.6 all-to-all-done.1
  322.9 10.9 %all-to-all-start.2 = ((f32[256,1,3,128]{3,1,2,0:T(1,128)}), f32[256,1,3,128]{3,1,2,0:T(1,128)S(1)}, u32[]{:S(2)}, u32[]{:S(2)}) async-start(f32[256,1,3,128]{3,1,2,0:T(1,128)} %stack.36), calls=%async_computation.2 | async-start | bytes 786432 | tf_op jit(solution)/shard_map/all_to_all | solution.py:24
  335.0 17.4 %all-to-all-done.2 = f32[256,1,3,128]{3,1,2,0:T(1,128)S(1)} async-done(((f32[256,1,3,128]{3,1,2,0:T(1,128)}), f32[256,1,3,128]{3,1,2,0:T(1,128)S(1)}, u32[]{:S(2)}, u32[]{:S(2)}) %all-to-all-start.2) | async-done | bytes 393248 | tf_op jit(solution)/shard_map/all_to_all | solution.py:24
  352.8 7.0 scatter_fusion
  364.3 6.9 psum.105
  371.4 11.3 %psum.106 = f32[3]{0:T(128)S(1)} all-reduce(f32[3]{0:T(128)S(1)} %psum.105), channel_id=1, replica_groups=mesh['blk_0'=4,'blk_1'=8,'blk_2'=2,'lat_0'=2,'lat_1'=2] {'blk_1'}, use_global_device_ids=true, to_apply=%region_7.8 | all-reduce | flops 3 | bytes 24 | tf_op jit(solution)/shard_map/psum | solution.py:56
  387.8 5.3 psum.108
  393.4 11.2 %psum.109 = f32[3]{0:T(128)S(1)} all-reduce(f32[3]{0:T(128)S(1)} %psum.108), channel_id=1, replica_groups=mesh['blk_0'=4,'blk_1'=8,'blk_2'=2,'lat_0'=2,'lat_1'=2] {'lat_1'}, use_global_device_ids=true, to_apply=%region_10.11 | all-reduce | flops 3 | bytes 24 | tf_op jit(solution)/shard_map/psum | solution.py:56
  404.7 4.1 scatter.101
  408.9 4.1 scatter.104
  413.0 8.9 %collective-permute-start.2 = (f32[3,5,5,1,1,128]{5,1,2,0,4,3:T(8,128)S(1)}, f32[3,5,5,1,1,128]{5,1,2,0,4,3:T(8,128)S(1)}, u32[]{:S(2)}, u32[]{:S(2)}) collective-permute-start(f32[3,5,5,1,1,128]{5,1,2,0,4,3:T(8,128)S(1)} %get-tuple-element.659), channel_id=1, source_target_pairs={{0,1},{1,2},{2,3},{4,5},{5,6},{6,7},{8,9},{9,10},{10,11},{12,13},{... | collective-permute-start | bytes 115208 | tf_op jit(solution)/shard_map/ppermute | solution.py:35
  425.2 5.7 collective-permute-done.3
  434.2 15.7 %all_to_all.45 = f32[64,4,3,10]{3,1,2,0:T(4,128)S(1)} all-to-all(f32[64,4,3,10]{3,1,2,0:T(4,128)S(1)} %copy.888), channel_id=1, replica_groups=mesh['blk_0'=4,'blk_1'=8,'blk_2'=2,'lat_0'=2,'lat_1'=2] {'blk_0','blk_1'..., dimensions={0} | all-to-all | bytes 61440 | tf_op jit(solution)/shard_map/all_to_all | solution.py:51
  450.8 5.0 all-to-all-start.4
  455.8 4.6 all-to-all-done.4
  461.5 5.9 all-to-all-start.5
  470.6 15.3 %all-to-all-done.5 = f32[256,1,3,128]{3,1,2,0:T(1,128)S(1)} async-done(((f32[256,1,3,128]{3,1,2,0:T(1,128)}), f32[256,1,3,128]{3,1,2,0:T(1,128)S(1)}, u32[]{:S(2)}, u32[]{:S(2)}) %all-to-all-start.5) | async-done | bytes 393248 | tf_op jit(solution)/shard_map/all_to_all | solution.py:24
  487.0 16.3 %scatter_fusion.1 = f32[256,3,128]{2,1,0:T(4,128)S(1)} fusion(f32[256,3,128]{2,1,0:T(4,128)S(1)} %broadcast.1226.clone.1, s32[256]{0:T(256)S(1)} %copy-done.40, f32[256,3,128]{2,1,0:T(4,128)} %copy.893), kind=kCustom, calls=%fused_computation.3 | custom fusion | bytes 1180672 | tf_op jit(solution)/shard_map/scatter | solution.py:305
  508.5 7.0 psum.110
  518.2 11.3 %psum.111 = f32[3]{0:T(128)S(1)} all-reduce(f32[3]{0:T(128)S(1)} %psum.110), channel_id=1, replica_groups=mesh['blk_0'=4,'blk_1'=8,'blk_2'=2,'lat_0'=2,'lat_1'=2] {'blk_1'}, use_global_device_ids=true, to_apply=%region_15.16 | all-reduce | flops 3 | bytes 24 | tf_op jit(solution)/shard_map/psum | solution.py:56
  531.0 4.1 psum.112
  536.7 5.4 psum.113
  544.5 10.4 %psum.114 = f32[3]{0:T(128)S(1)} all-reduce(f32[3]{0:T(128)S(1)} %psum.113), channel_id=1, replica_groups=mesh['blk_0'=4,'blk_1'=8,'blk_2'=2,'lat_0'=2,'lat_1'=2] {'lat_1'}, use_global_device_ids=true, to_apply=%region_18.19 | all-reduce | flops 3 | bytes 24 | tf_op jit(solution)/shard_map/psum | solution.py:56
  560.0 6.1 collective-permute-done.8
  566.2 4.0 scatter.124
  570.2 4.0 scatter.125
  574.3 4.6 collective-permute-start.10
  581.0 5.0 collective-permute-done.11
  591.2 4.6 all-to-all-start.6
  596.6 11.2 %all-to-all-done.6 = f32[64,4,3,10]{3,1,2,0:T(4,128)S(1)} async-done(((f32[64,4,3,10]{3,1,2,0:T(4,128)}), f32[64,4,3,10]{3,1,2,0:T(4,128)S(1)}, u32[]{:S(2)}, u32[]{:S(2)}) %all-to-all-start.6) | async-done | bytes 30752 | tf_op jit(solution)/shard_map/all_to_all | solution.py:51
  617.5 7.5 %all-to-all-start.8 = ((f32[256,1,3,128]{3,1,2,0:T(1,128)}), f32[256,1,3,128]{3,1,2,0:T(1,128)}, u32[]{:S(2)}, u32[]{:S(2)}) async-start(f32[256,1,3,128]{3,1,2,0:T(1,128)} %stack.38), calls=%async_computation.8 | async-start | bytes 786432 | tf_op jit(solution)/shard_map/all_to_all | solution.py:24
  628.5 14.0 %all-to-all-done.8 = f32[256,1,3,128]{3,1,2,0:T(1,128)} async-done(((f32[256,1,3,128]{3,1,2,0:T(1,128)}), f32[256,1,3,128]{3,1,2,0:T(1,128)}, u32[]{:S(2)}, u32[]{:S(2)}) %all-to-all-start.8) | async-done | bytes 393248 | tf_op jit(solution)/shard_map/all_to_all | solution.py:24
  644.8 16.3 %scatter_fusion.2 = f32[256,3,128]{2,1,0:T(4,128)S(1)} fusion(f32[256,3,128]{2,1,0:T(4,128)S(1)} %broadcast.1226, s32[256]{0:T(256)S(1)} %copy-done.41, f32[256,3,128]{2,1,0:T(4,128)} %copy.928), kind=kCustom, calls=%fused_computation.4 | custom fusion | bytes 1180672 | tf_op jit(solution)/shard_map/scatter | solution.py:305
  665.9 6.9 psum.115
  674.3 11.6 %psum.116 = f32[3]{0:T(128)S(1)} all-reduce(f32[3]{0:T(128)S(1)} %psum.115), channel_id=1, replica_groups=mesh['blk_0'=4,'blk_1'=8,'blk_2'=2,'lat_0'=2,'lat_1'=2] {'blk_1'}, use_global_device_ids=true, to_apply=%region_23.24 | all-reduce | flops 3 | bytes 24 | tf_op jit(solution)/shard_map/psum | solution.py:56
  687.8 3.8 psum.117
  691.7 5.3 psum.118
  697.7 10.6 %psum.119 = f32[3]{0:T(128)S(1)} all-reduce(f32[3]{0:T(128)S(1)} %psum.118), channel_id=1, replica_groups=mesh['blk_0'=4,'blk_1'=8,'blk_2'=2,'lat_0'=2,'lat_1'=2] {'lat_1'}, use_global_device_ids=true, to_apply=%region_26.27 | all-reduce | flops 3 | bytes 24 | tf_op jit(solution)/shard_map/psum | solution.py:56
  713.1 5.8 collective-permute-done.12
  719.0 4.0 scatter.162
  723.0 4.0 scatter.163
  727.0 4.9 collective-permute-start.14
  734.0 5.0 collective-permute-done.15
  (1530 shorter events, 301.8 us)
Async XLA Ops:
  0.6 30.8 %copy-start.17 = (f32[5,5,1,1,1,1]{1,0,5,4,3,2:T(8,128)S(1)}, f32[5,5,1,1,1,1]{1,0,5,4,3,2:T(8,128)}, u32[]{:S(2)}) copy-start(f32[5,5,1,1,1,1]{1,0,5,4,3,2:T(8,128)} %constant.794) | copy-start | bytes 304
  0.6 30.8 %copy-start = (f32[3,5,5,5,1,2,128]{6,5,4,3,2,1,0:T(2,128)S(1)}, f32[3,5,5,5,1,2,128]{6,5,4,3,2,1,0:T(2,128)}, u32[]{:S(2)}) copy-start(f32[3,5,5,5,1,2,128]{6,5,4,3,2,1,0:T(2,128)} %param.74) | copy-start | bytes 1152004
  4.7 296.2 %collective-permute-start.4 = (f32[1,5,5,1,2,128]{5,4,2,1,3,0:T(2,128)}, f32[1,5,5,1,2,128]{5,4,2,1,3,0:T(2,128)}, u32[]{:S(2)}, u32[]{:S(2)}) collective-permute-start(f32[1,5,5,1,2,128]{5,4,2,1,3,0:T(2,128)} %get-tuple-element.646), channel_id=1, source_target_pairs={{0,4},{4,8},{8,12},{12,16},{16,20},{20,24},{24,28},{28,32},{32,36}... | collective-permute-start | bytes 76808 | tf_op jit(solution)/shard_map/ppermute | solution.py:35
  6.8 294.9 %collective-permute-start.5 = (f32[1,5,5,1,2,128]{5,4,2,1,3,0:T(2,128)}, f32[1,5,5,1,2,128]{5,4,2,1,3,0:T(2,128)}, u32[]{:S(2)}, u32[]{:S(2)}) collective-permute-start(f32[1,5,5,1,2,128]{5,4,2,1,3,0:T(2,128)} %get-tuple-element.645), channel_id=1, source_target_pairs={{4,0},{8,4},{12,8},{16,12},{20,16},{24,20},{28,24},{32,28},{36,32}... | collective-permute-start | bytes 76808 | tf_op jit(solution)/shard_map/ppermute | solution.py:38
  25.0 285.8 %all-to-all-start = ((f32[64,4,3,10]{3,1,2,0:T(4,128)}), f32[64,4,3,10]{3,1,2,0:T(4,128)S(1)}, u32[]{:S(2)}, u32[]{:S(2)}) async-start(f32[64,4,3,10]{3,1,2,0:T(4,128)} %copy.834), calls=%async_computation | async-start | bytes 786432 | tf_op jit(solution)/shard_map/all_to_all | solution.py:51
  298.6 23.3 %copy-start.9 = (f32[64,3,3,128]{3,0,2,1:T(8,128)S(1)}, f32[64,3,3,128]{3,0,2,1:T(8,128)}, u32[]{:S(2)}) copy-start(f32[64,3,3,128]{3,0,2,1:T(8,128)} %param.79) | copy-start | bytes 884740
  298.7 24.3 %copy-start.18 = (f32[1,63,3,128]{3,1,2,0:T(8,128)}, f32[1,63,3,128]{3,1,2,0:T(8,128)S(1)}, u32[]{:S(2)}) copy-start(f32[1,63,3,128]{3,1,2,0:T(8,128)S(1)} %copy.838) | copy-start | bytes 290308
  302.5 8.2 %collective-permute-start.6 = (f32[1,5,5,1,1,128]{5,4,3,2,1,0:T(1,128)S(1)}, f32[1,5,5,1,1,128]{5,4,3,2,1,0:T(1,128)S(1)}, u32[]{:S(2)}, u32[]{:S(2)}) collective-permute-start(f32[1,5,5,1,1,128]{5,4,3,2,1,0:T(1,128)S(1)} %get-tuple-element.665), channel_id=1, source_target_pairs={{0,1},{1,2},{2,3},{4,5},{5,6},{6,7},{8,9},{9,10},{10,11},{12,13},{... | collective-permute-start | bytes 38408 | tf_op jit(solution)/shard_map/ppermute | solution.py:35
  308.8 8.4 %collective-permute-start.7 = (f32[1,5,5,1,1,128]{5,4,3,2,1,0:T(1,128)S(1)}, f32[1,5,5,1,1,128]{5,4,3,2,1,0:T(1,128)S(1)}, u32[]{:S(2)}, u32[]{:S(2)}) collective-permute-start(f32[1,5,5,1,1,128]{5,4,3,2,1,0:T(1,128)S(1)} %get-tuple-element.664), channel_id=1, source_target_pairs={{1,0},{2,1},{3,2},{5,4},{6,5},{7,6},{9,8},{10,9},{11,10},{13,12},{... | collective-permute-start | bytes 38408 | tf_op jit(solution)/shard_map/ppermute | solution.py:38
  312.3 9.5 %all-to-all-start.1 = ((f32[4,1,3,128]{3,1,2,0:T(1,128)}), f32[4,1,3,128]{3,1,2,0:T(1,128)S(1)}, u32[]{:S(2)}, u32[]{:S(2)}) async-start(f32[4,1,3,128]{3,1,2,0:T(1,128)} %copy.837), calls=%async_computation.1 | async-start | bytes 12288 | tf_op jit(solution)/shard_map/all_to_all | solution.py:51
  321.9 30.8 %copy-start.44 = (f32[1,1,3,128]{3,1,2,0:T(1,128)}, f32[1,1,3,128]{3,1,2,0:T(1,128)S(1)}, u32[]{:S(2)}) copy-start(f32[1,1,3,128]{3,1,2,0:T(1,128)S(1)} %broadcast_in_dim.181) | copy-start | bytes 4612
  322.9 29.8 %copy-start.39 = (s32[256]{0:T(256)S(1)}, s32[256]{0:T(256)}, u32[]{:S(2)}) copy-start(s32[256]{0:T(256)} %copy-done.38) | copy-start | bytes 3076
  322.9 29.4 %all-to-all-start.2 = ((f32[256,1,3,128]{3,1,2,0:T(1,128)}), f32[256,1,3,128]{3,1,2,0:T(1,128)S(1)}, u32[]{:S(2)}, u32[]{:S(2)}) async-start(f32[256,1,3,128]{3,1,2,0:T(1,128)} %stack.36), calls=%async_computation.2 | async-start | bytes 786432 | tf_op jit(solution)/shard_map/all_to_all | solution.py:24
  359.8 44.8 %copy-start.57 = (f32[3]{0:T(128)S(1)}, f32[3]{0:T(128)}, u32[]{:S(2)}) copy-start(f32[3]{0:T(128)} %param.81) | copy-start | bytes 40
  359.8 44.8 %copy-start.58 = (f32[3]{0:T(128)S(1)}, f32[3]{0:T(128)}, u32[]{:S(2)}) copy-start(f32[3]{0:T(128)} %param.82) | copy-start | bytes 40
  386.6 22.2 %collective-permute-start.1 = (f32[3,5,5,1,2,128]{5,4,2,1,0,3:T(2,128)S(1)}, f32[3,5,5,1,2,128]{5,4,2,1,0,3:T(2,128)S(1)}, u32[]{:S(2)}, u32[]{:S(2)}) collective-permute-start(f32[3,5,5,1,2,128]{5,4,2,1,0,3:T(2,128)S(1)} %bitcast.576), channel_id=1, source_target_pairs={{4,0},{8,4},{12,8},{16,12},{20,16},{24,20},{28,24},{32,28},{36,32}... | collective-permute-start | bytes 230408 | tf_op jit(solution)/shard_map/ppermute | solution.py:38
  393.0 11.6 %collective-permute-start = (f32[3,5,5,1,2,128]{5,4,2,1,0,3:T(2,128)S(1)}, f32[3,5,5,1,2,128]{5,4,2,1,0,3:T(2,128)S(1)}, u32[]{:S(2)}, u32[]{:S(2)}) collective-permute-start(f32[3,5,5,1,2,128]{5,4,2,1,0,3:T(2,128)S(1)} %bitcast.574), channel_id=1, source_target_pairs={{0,4},{4,8},{8,12},{12,16},{16,20},{20,24},{24,28},{28,32},{32,36}... | collective-permute-start | bytes 230408 | tf_op jit(solution)/shard_map/ppermute | solution.py:35
  404.6 26.3 %copy-start.50 = (f32[3]{0:T(128)}, f32[3]{0:T(128)S(1)}, u32[]{:S(2)}) copy-start(f32[3]{0:T(128)S(1)} %multiply_add_fusion.8) | copy-start | bytes 40
  413.0 10.2 %collective-permute-start.2 = (f32[3,5,5,1,1,128]{5,1,2,0,4,3:T(8,128)S(1)}, f32[3,5,5,1,1,128]{5,1,2,0,4,3:T(8,128)S(1)}, u32[]{:S(2)}, u32[]{:S(2)}) collective-permute-start(f32[3,5,5,1,1,128]{5,1,2,0,4,3:T(8,128)S(1)} %get-tuple-element.659), channel_id=1, source_target_pairs={{0,1},{1,2},{2,3},{4,5},{5,6},{6,7},{8,9},{9,10},{10,11},{12,13},{... | collective-permute-start | bytes 115208 | tf_op jit(solution)/shard_map/ppermute | solution.py:35
  423.3 7.7 %collective-permute-start.3 = (f32[3,5,5,1,1,128]{5,1,2,0,4,3:T(8,128)S(1)}, f32[3,5,5,1,1,128]{5,1,2,0,4,3:T(8,128)S(1)}, u32[]{:S(2)}, u32[]{:S(2)}) collective-permute-start(f32[3,5,5,1,1,128]{5,1,2,0,4,3:T(8,128)S(1)} %get-tuple-element.656), channel_id=1, source_target_pairs={{1,0},{2,1},{3,2},{5,4},{6,5},{7,6},{9,8},{10,9},{11,10},{13,12},{... | collective-permute-start | bytes 115208 | tf_op jit(solution)/shard_map/ppermute | solution.py:38
  431.5 24.3 %copy-start.19 = (f32[1,63,3,128]{3,1,2,0:T(8,128)S(1)}, f32[1,63,3,128]{3,1,2,0:T(8,128)}, u32[]{:S(2)}) copy-start(f32[1,63,3,128]{3,1,2,0:T(8,128)} %copy-done.18) | copy-start | bytes 290308
  431.5 24.3 %copy-start.45 = (f32[1,1,3,128]{3,1,2,0:T(1,128)S(1)}, f32[1,1,3,128]{3,1,2,0:T(1,128)}, u32[]{:S(2)}) copy-start(f32[1,1,3,128]{3,1,2,0:T(1,128)} %copy-done.44) | copy-start | bytes 4612
  431.5 28.9 %copy-start.10 = (f32[64,3,3,128]{3,0,2,1:T(8,128)S(1)}, f32[64,3,3,128]{3,0,2,1:T(8,128)}, u32[]{:S(2)}) copy-start(f32[64,3,3,128]{3,0,2,1:T(8,128)} %param.79) | copy-start | bytes 884740
  450.8 9.6 %all-to-all-start.4 = ((f32[4,1,3,128]{3,1,2,0:T(1,128)}), f32[4,1,3,128]{3,1,2,0:T(1,128)S(1)}, u32[]{:S(2)}, u32[]{:S(2)}) async-start(f32[4,1,3,128]{3,1,2,0:T(1,128)} %copy.891), calls=%async_computation.4 | async-start | bytes 12288 | tf_op jit(solution)/shard_map/all_to_all | solution.py:51
  461.5 24.4 %all-to-all-start.5 = ((f32[256,1,3,128]{3,1,2,0:T(1,128)}), f32[256,1,3,128]{3,1,2,0:T(1,128)S(1)}, u32[]{:S(2)}, u32[]{:S(2)}) async-start(f32[256,1,3,128]{3,1,2,0:T(1,128)} %stack.37), calls=%async_computation.5 | async-start | bytes 786432 | tf_op jit(solution)/shard_map/all_to_all | solution.py:24
  508.5 33.6 %copy-start.42 = (f32[5,5,1,1,1,1]{1,0,2,4,5,3:T(8,128)S(1)}, f32[5,5,1,1,1,1]{1,0,2,4,5,3:T(8,128)}, u32[]{:S(2)}) copy-start(f32[5,5,1,1,1,1]{1,0,2,4,5,3:T(8,128)} %constant.795) | copy-start | bytes 304
  531.0 23.8 %copy-start.59 = (f32[3]{0:T(128)S(1)}, f32[3]{0:T(128)}, u32[]{:S(2)}) copy-start(f32[3]{0:T(128)} %param.82) | copy-start | bytes 40
  531.0 23.8 %copy-start.61 = (f32[3]{0:T(128)S(1)}, f32[3]{0:T(128)}, u32[]{:S(2)}) copy-start(f32[3]{0:T(128)} %copy-done.60) | copy-start | bytes 40
  536.7 21.1 %copy-start.51 = (f32[3]{0:T(128)S(1)}, f32[3]{0:T(128)}, u32[]{:S(2)}) copy-start(f32[3]{0:T(128)} %copy-done.50) | copy-start | bytes 40
  556.2 3.7 collective-permute-start.9
  558.6 7.5 %collective-permute-start.8 = (f32[3,5,5,1,2,128]{5,4,2,1,0,3:T(2,128)S(1)}, f32[3,5,5,1,2,128]{5,4,2,1,0,3:T(2,128)S(1)}, u32[]{:S(2)}, u32[]{:S(2)}) collective-permute-start(f32[3,5,5,1,2,128]{5,4,2,1,0,3:T(2,128)S(1)} %bitcast.582), channel_id=1, source_target_pairs={{0,4},{4,8},{8,12},{12,16},{16,20},{20,24},{24,28},{28,32},{32,36}... | collective-permute-start | bytes 230408 | tf_op jit(solution)/shard_map/ppermute | solution.py:35
  574.3 6.6 collective-permute-start.10
  578.9 7.0 collective-permute-start.11
  587.9 20.1 %copy-start.49 = (pred[4]{0:T(512)(128)(4,1)S(1)}, pred[4]{0:T(512)(128)(4,1)}, u32[]{:S(2)}) copy-start(pred[4]{0:T(512)(128)(4,1)} %get-tuple-element.606) | copy-start | bytes 16
  589.0 27.5 %copy-start.11 = (f32[64,3,3,128]{3,0,2,1:T(8,128)S(1)}, f32[64,3,3,128]{3,0,2,1:T(8,128)}, u32[]{:S(2)}) copy-start(f32[64,3,3,128]{3,0,2,1:T(8,128)} %param.79) | copy-start | bytes 884740
  591.2 16.6 %all-to-all-start.6 = ((f32[64,4,3,10]{3,1,2,0:T(4,128)}), f32[64,4,3,10]{3,1,2,0:T(4,128)S(1)}, u32[]{:S(2)}, u32[]{:S(2)}) async-start(f32[64,4,3,10]{3,1,2,0:T(4,128)} %copy.923), calls=%async_computation.6 | async-start | bytes 786432 | tf_op jit(solution)/shard_map/all_to_all | solution.py:51
  608.8 6.7 all-to-all-start.7
  617.5 25.1 %all-to-all-start.8 = ((f32[256,1,3,128]{3,1,2,0:T(1,128)}), f32[256,1,3,128]{3,1,2,0:T(1,128)}, u32[]{:S(2)}, u32[]{:S(2)}) async-start(f32[256,1,3,128]{3,1,2,0:T(1,128)} %stack.38), calls=%async_computation.8 | async-start | bytes 786432 | tf_op jit(solution)/shard_map/all_to_all | solution.py:24
  644.8 20.0 %copy-start.37 = (f32[3,3,10,5]{2,1,3,0:T(4,128)S(1)}, f32[3,3,10,5]{2,1,3,0:T(4,128)}, u32[]{:S(2)}) copy-start(f32[3,3,10,5]{2,1,3,0:T(4,128)} %get-tuple-element.661) | copy-start | bytes 5404
  664.5 21.3 %copy-start.12 = (f32[3,5,5,2,128,5]{4,5,3,2,1,0:T(8,128)S(1)}, f32[3,5,5,2,128,5]{4,5,3,2,1,0:T(8,128)}, u32[]{:S(2)}) copy-start(f32[3,5,5,2,128,5]{4,5,3,2,1,0:T(8,128)} %fusion.49) | copy-start | bytes 1152004
  664.5 21.3 %copy-start.43 = (f32[5,5,1,1,1,1]{1,0,2,4,5,3:T(8,128)S(1)}, f32[5,5,1,1,1,1]{1,0,2,4,5,3:T(8,128)}, u32[]{:S(2)}) copy-start(f32[5,5,1,1,1,1]{1,0,2,4,5,3:T(8,128)} %constant.795) | copy-start | bytes 304
  665.9 25.8 %copy-start.22 = (f32[1,63,3,128]{3,1,2,0:T(8,128)S(1)}, f32[1,63,3,128]{3,1,2,0:T(8,128)}, u32[]{:S(2)}) copy-start(f32[1,63,3,128]{3,1,2,0:T(8,128)} %fusion.97) | copy-start | bytes 290308
  674.3 36.3 %copy-start.52 = (f32[3]{0:T(128)S(1)}, f32[3]{0:T(128)}, u32[]{:S(2)}) copy-start(f32[3]{0:T(128)} %copy-done.50) | copy-start | bytes 40
  674.3 36.3 %copy-start.55 = (f32[3]{0:T(128)S(1)}, f32[3]{0:T(128)}, u32[]{:S(2)}) copy-start(f32[3]{0:T(128)} %copy-done.54) | copy-start | bytes 40
  709.3 3.7 collective-permute-start.13
  711.2 7.7 %collective-permute-start.12 = (f32[3,5,5,1,2,128]{5,4,2,1,0,3:T(2,128)S(1)}, f32[3,5,5,1,2,128]{5,4,2,1,0,3:T(2,128)S(1)}, u32[]{:S(2)}, u32[]{:S(2)}) collective-permute-start(f32[3,5,5,1,2,128]{5,4,2,1,0,3:T(2,128)S(1)} %bitcast.583), channel_id=1, source_target_pairs={{0,4},{4,8},{8,12},{12,16},{16,20},{20,24},{24,28},{28,32},{32,36}... | collective-permute-start | bytes 230408 | tf_op jit(solution)/shard_map/ppermute | solution.py:35
  727.0 6.8 collective-permute-start.14
  731.9 7.0 collective-permute-start.15
  (39 other events, 387.5 us)
